TPU v7x, 32 devices: a whole 2x2x4 slice. The times are simulated.
32 devices in a mesh: seq: 8 (over z, x), heads: 2 (over core), dp: 2 (over y).
Axes of the slice: x: 2, y: 2, z: 4, core: 2. Of those that a mesh axis runs over, the one named last changes fastest.
Arguments:
- queries: bfloat16 [2048, 2048], P(('dp', 'seq'), 'heads'), parts along dimension 0, may hold values from -6 to 6
- keys: bfloat16 [2048, 512], P(('dp', 'seq'), 'heads'), parts along dimension 0, may hold values from -6 to 6
- values: bfloat16 [2048, 512], P(('dp', 'seq'), 'heads'), parts along dimension 0, may hold values from -6 to 6
- house: bfloat16 [2048, 512], P(('dp', 'seq'), 'heads'), parts along dimension 0, may hold values from -16 to 16
- beta: float32 [4, 2048], P('heads', ('dp', 'seq')), parts along dimension 1, may hold values from 0.5 to 1.5
- out_weight: bfloat16 [2048, 2048], P('heads'), may hold values from -2 to 2
Outputs:
- mixed: bfloat16 [2048, 2048], P(('dp', 'seq'), 'heads'), parts along dimension 0
There are 2 independent parts, one for each index of `dp`. A program takes and returns all parts, laid end to end along the dimension named above; an argument that names none is the same for every part. Nothing has to cross between parts.
All inputs are finite; a program needn't handle non-finite values.
Results may differ from a plain program's by a relative error of at most 0.012.
Values may be sent and summed in bfloat16 or wider, within the bound.
A program may use at most 64 MiB of HBM per device.

v0:
```python
import math

import jax
import jax.numpy as jnp
from jax import lax
from jax.sharding import PartitionSpec as P

HD = 128


highest = lax.Precision.HIGHEST
norm_floor = 1e-06
masked_score = -1e30


def shifted(value, axis, by):
    devices = lax.axis_size(axis)
    pairs = [(i, i + by) for i in range(devices) if 0 <= i + by < devices]
    return lax.ppermute(value, axis, pairs)


def unit_vectors(house_rows):
    return house_rows / jnp.sqrt(
        jnp.sum(house_rows * house_rows, axis=-1, keepdims=True) + norm_floor
    )


def lower_solve(matrix, right):
    return lax.linalg.triangular_solve(matrix, right, left_side=True, lower=True)


def lower_solve_flipped(matrix, right):
    return lax.linalg.triangular_solve(matrix, right, left_side=True, lower=True, transpose_a=True)


def block_local(query_rows, key_rows, vectors, betas):
    rows_dev, groups, per_group, head_size = query_rows.shape
    offsets = jnp.arange(rows_dev, dtype=jnp.int32)
    upto = (offsets[None, :] <= offsets[:, None]).astype(jnp.float32)
    below = (offsets[None, :] < offsets[:, None]).astype(jnp.float32)
    inner = jnp.einsum("agd,bgd->gab", vectors, vectors, precision=highest)
    diagonal = jnp.eye(rows_dev, dtype=jnp.float32)[None] * (1.0 / jnp.transpose(betas))[:, :, None]
    inverse_factor = inner * below[None] + diagonal
    query_along = (
        jnp.einsum("tgqd,agd->gtqa", query_rows, vectors, precision=highest)
        * upto[None, :, None, :]
    )
    key_along = jnp.einsum("bgd,jgd->gbj", vectors, key_rows, precision=highest) * below[None]
    plain = jnp.einsum("tgqd,jgd->gtqj", query_rows, key_rows, precision=highest)
    solved_keys = jax.vmap(lower_solve)(inverse_factor, key_along)
    flat_along = jnp.transpose(
        query_along.reshape(groups, rows_dev * per_group, rows_dev), (0, 2, 1)
    )
    solved_queries = jax.vmap(lower_solve_flipped)(inverse_factor, flat_along)
    solved_queries = jnp.transpose(solved_queries, (0, 2, 1)).reshape(
        groups, rows_dev, per_group, rows_dev
    )
    scores = plain - jnp.einsum("gtqa,gaj->gtqj", query_along, solved_keys, precision=highest)
    scores = jnp.transpose(scores, (1, 0, 2, 3))
    turned = query_rows - jnp.einsum("gtqb,bgd->tgqd", solved_queries, vectors, precision=highest)
    block_ends = key_rows - jnp.einsum("gaj,agd->jgd", solved_keys, vectors, precision=highest)
    solved_vectors = jax.vmap(lower_solve)(inverse_factor, jnp.transpose(vectors, (1, 0, 2)))
    product = jnp.eye(head_size, dtype=jnp.float32)[None] - jnp.einsum(
        "agd,gae->gde", vectors, solved_vectors, precision=highest
    )
    return (scores, turned, block_ends, product)


def per_device(queries, keys, values, house, beta, out_weight):
    rows_dev = queries.shape[0]
    groups = keys.shape[1] // HD
    per_group = queries.shape[1] // keys.shape[1]
    score_scale = 1.0 / math.sqrt(HD)
    my_block = lax.axis_index("seq")
    cycle_size = lax.axis_size("seq")
    query_rows = queries.astype(jnp.float32).reshape(rows_dev, groups, per_group, HD)
    key_rows = keys.astype(jnp.float32).reshape(rows_dev, groups, HD)
    vector_rows = unit_vectors(house.astype(jnp.float32).reshape(rows_dev, groups, HD))
    scores, turned, ends_float, product = block_local(
        query_rows, key_rows, vector_rows, jnp.transpose(beta)
    )
    offsets = jnp.arange(rows_dev, dtype=jnp.int32)
    causal = offsets[None, :] <= offsets[:, None]
    local_scores = jnp.where(causal[:, None, None, :], scores * score_scale, masked_score)
    row_max = jnp.max(local_scores, axis=-1, keepdims=True)
    near_weights = jnp.exp(local_scores - row_max)
    row_total = jnp.sum(near_weights, axis=-1, keepdims=True)
    value_rows = values.reshape(rows_dev, groups, HD)
    weighted = jnp.einsum(
        "tgqj,jgd->tgqd",
        near_weights.astype(jnp.bfloat16),
        value_rows,
        preferred_element_type=jnp.float32,
    )
    near_queries = turned.astype(jnp.bfloat16)
    block_ends = ends_float.astype(jnp.bfloat16)
    block_map = product.astype(jnp.bfloat16)

    def absorb(softmax_state, far_keys, far_values, usable):
        old_max, old_total, old_weighted = softmax_state
        far_scores = (
            jnp.einsum("tgqd,jgd->tgqj", near_queries, far_keys, preferred_element_type=jnp.float32)
            * score_scale
        )
        far_scores = jnp.where(usable, far_scores, masked_score)
        new_max = jnp.maximum(old_max, jnp.max(far_scores, axis=-1, keepdims=True))
        shrink = jnp.exp(old_max - new_max)
        far_weights = jnp.exp(far_scores - new_max)
        new_total = old_total * shrink + jnp.sum(far_weights, axis=-1, keepdims=True)
        new_weighted = old_weighted * shrink + jnp.einsum(
            "tgqj,jgd->tgqd",
            far_weights.astype(jnp.bfloat16),
            far_values,
            preferred_element_type=jnp.float32,
        )
        return (new_max, new_total, new_weighted)

    softmax_state = (row_max, row_total, weighted)
    map_float = block_map.astype(jnp.float32)

    def cycle_step(step_index, loop_carry):
        current_state, outgoing = loop_carry
        received = shifted(outgoing, "seq", 1)
        far_keys = received[0].reshape(rows_dev, groups, HD)
        far_values = received[1].reshape(rows_dev, groups, HD).astype(jnp.bfloat16)
        current_state = absorb(
            current_state, far_keys.astype(jnp.bfloat16), far_values, step_index <= my_block
        )
        forward = jnp.einsum("gba,jga->jgb", map_float, far_keys, precision=highest)
        outgoing = jnp.stack([forward.reshape(rows_dev, groups * HD), received[1]])
        return (current_state, outgoing)

    outgoing = jnp.stack(
        [block_ends.astype(jnp.float32).reshape(rows_dev, groups * HD), values.astype(jnp.float32)]
    )
    softmax_state = lax.fori_loop(1, cycle_size, cycle_step, (softmax_state, outgoing))[0]
    final_max, final_total, final_weighted = softmax_state
    attended = (
        (final_weighted / final_total)
        .astype(jnp.bfloat16)
        .reshape(rows_dev, groups * per_group * HD)
    )
    partial_out = jnp.dot(attended, out_weight, preferred_element_type=jnp.float32)
    return lax.psum_scatter(
        partial_out.astype(jnp.bfloat16), "heads", scatter_dimension=1, tiled=True
    )


def solution(mesh):
    in_specs = (
        P(("dp", "seq"), "heads"),
        P(("dp", "seq"), "heads"),
        P(("dp", "seq"), "heads"),
        P(("dp", "seq"), "heads"),
        P("heads", ("dp", "seq")),
        P("heads", None),
    )
    out_specs = P(("dp", "seq"), "heads")
    return jax.shard_map(
        per_device, mesh=mesh, in_specs=in_specs, out_specs=out_specs, check_vma=False
    )
```

profile of v0, /device:TPU:25, one launch (start us, length us, event | category | flops | bytes accessed | tf_op | source)
XLA Modules:
  0.0 134.2 jit_solution(5475112373903814050)
XLA Ops:
  6.6 0.9 reshape.108
  7.5 1.0 copy.136
  8.4 1.0 copy.123
  9.4 0.1 copy.174
  9.6 0.1 copy.126
  9.8 0.7 broadcast_divide_fusion.1
  10.5 0.5 fusion.19
  10.9 19.7 %custom-call.8 = f32[2,1,128,128]{2,3,1,0:T(8,128)S(1)} custom-call(f32[2,1,128,128]{3,2,1,0:T(8,128)S(1)} %fusion.19), custom_call_target="InvertDiagBlocksLowerTriangular" | custom-call | tf_op jit(solution)/shard_map/vmap()/triangular_solve/custom-call.1 | solution.py:29
  30.6 1.0 copy.120
  31.6 0.3 convolution_multiply_fusion.1
  31.9 1.1 copy.119
  33.1 0.4 fusion.37
  33.5 0.5 fusion.21
  33.9 0.5 fusion.10
  34.5 0.6 fusion.28
  35.1 0.3 copy.137
  35.4 0.4 fusion.32
  35.9 0.3 fusion.45
  36.3 0.3 convolution_bitcast_fusion.2
  36.6 0.6 fusion.35
  37.2 0.7 fusion.15
  37.9 0.2 copy.144
  38.1 0.5 fusion.22
  38.6 68.3 %while.19 = (s32[]{:T(128)}, f32[128,2,4,1]{0,2,1,3:T(4,128)S(1)}, f32[128,2,4,1]{0,2,1,3:T(4,128)S(1)}, f32[128,2,4,128]{3,0,2,1:T(8,128)S(1)}, f32[2,128,256]{...) while((s32[]{:T(128)}, f32[128,2,4,1]{0,2,1,3:T(4,128)S(1)}, ...), condition=%wide.region_6.8_spmd, body=%wide.region_3.7_spmd.sunk | while | flops 118688768 | bytes 5898383 | solution.py:136
  38.6 3.1 %collective-permute-start = (f32[2,128,256]{1,2,0:T(8,128)S(1)}, f32[2,128,256]{1,2,0:T(8,128)S(1)}, u32[]{:S(2)}, u32[]{:S(2)}) collective-permute-start(f32[2,128,256]{1,2,0:T(8,128)S(1)} %get-tuple-element.288), channel_id=1, source_target_pairs={{0,4},{4,8},{8,12},{12,16},{16,20},{20,24},{24,28},{1,5},{5,9},{9,... | collective-permute-start | bytes 786440 | tf_op jit(solution)/shard_map/while/body/eval_jaxpr/ppermute | solution.py:19
  41.7 6.8 %collective-permute-done = f32[2,128,256]{1,2,0:T(8,128)S(1)} collective-permute-done((f32[2,128,256]{1,2,0:T(8,128)S(1)}, f32[2,128,256]{1,2,0:T(8,128)S(1)}, u32[]{:S(2)}, u32[]{:S(2)}) %collective-permute-start) | collective-permute-done | bytes 262176 | tf_op jit(solution)/shard_map/while/body/eval_jaxpr/ppermute | solution.py:19
  48.6 0.1 copy.180
  48.7 0.3 fusion.79
  49.1 0.3 fusion.83
  49.4 0.4 fusion.82
  49.9 2.2 %collective-permute-start = (f32[2,128,256]{1,2,0:T(8,128)S(1)}, f32[2,128,256]{1,2,0:T(8,128)S(1)}, u32[]{:S(2)}, u32[]{:S(2)}) collective-permute-start(f32[2,128,256]{1,2,0:T(8,128)S(1)} %get-tuple-element.288), channel_id=1, source_target_pairs={{0,4},{4,8},{8,12},{12,16},{16,20},{20,24},{24,28},{1,5},{5,9},{9,... | collective-permute-start | bytes 786440 | tf_op jit(solution)/shard_map/while/body/eval_jaxpr/ppermute | solution.py:19
  52.1 6.8 %collective-permute-done = f32[2,128,256]{1,2,0:T(8,128)S(1)} collective-permute-done((f32[2,128,256]{1,2,0:T(8,128)S(1)}, f32[2,128,256]{1,2,0:T(8,128)S(1)}, u32[]{:S(2)}, u32[]{:S(2)}) %collective-permute-start) | collective-permute-done | bytes 262176 | tf_op jit(solution)/shard_map/while/body/eval_jaxpr/ppermute | solution.py:19
  59.0 0.3 fusion.79
  59.4 0.3 fusion.83
  59.8 0.4 fusion.82
  60.2 1.9 %collective-permute-start = (f32[2,128,256]{1,2,0:T(8,128)S(1)}, f32[2,128,256]{1,2,0:T(8,128)S(1)}, u32[]{:S(2)}, u32[]{:S(2)}) collective-permute-start(f32[2,128,256]{1,2,0:T(8,128)S(1)} %get-tuple-element.288), channel_id=1, source_target_pairs={{0,4},{4,8},{8,12},{12,16},{16,20},{20,24},{24,28},{1,5},{5,9},{9,... | collective-permute-start | bytes 786440 | tf_op jit(solution)/shard_map/while/body/eval_jaxpr/ppermute | solution.py:19
  62.2 6.1 %collective-permute-done = f32[2,128,256]{1,2,0:T(8,128)S(1)} collective-permute-done((f32[2,128,256]{1,2,0:T(8,128)S(1)}, f32[2,128,256]{1,2,0:T(8,128)S(1)}, u32[]{:S(2)}, u32[]{:S(2)}) %collective-permute-start) | collective-permute-done | bytes 262176 | tf_op jit(solution)/shard_map/while/body/eval_jaxpr/ppermute | solution.py:19
  68.4 0.2 fusion.79
  68.8 0.3 fusion.83
  69.1 0.4 fusion.82
  69.6 1.9 %collective-permute-start = (f32[2,128,256]{1,2,0:T(8,128)S(1)}, f32[2,128,256]{1,2,0:T(8,128)S(1)}, u32[]{:S(2)}, u32[]{:S(2)}) collective-permute-start(f32[2,128,256]{1,2,0:T(8,128)S(1)} %get-tuple-element.288), channel_id=1, source_target_pairs={{0,4},{4,8},{8,12},{12,16},{16,20},{20,24},{24,28},{1,5},{5,9},{9,... | collective-permute-start | bytes 786440 | tf_op jit(solution)/shard_map/while/body/eval_jaxpr/ppermute | solution.py:19
  71.5 6.1 %collective-permute-done = f32[2,128,256]{1,2,0:T(8,128)S(1)} collective-permute-done((f32[2,128,256]{1,2,0:T(8,128)S(1)}, f32[2,128,256]{1,2,0:T(8,128)S(1)}, u32[]{:S(2)}, u32[]{:S(2)}) %collective-permute-start) | collective-permute-done | bytes 262176 | tf_op jit(solution)/shard_map/while/body/eval_jaxpr/ppermute | solution.py:19
  77.6 0.1 copy.180
  77.7 0.2 fusion.79
  78.1 0.3 fusion.83
  78.4 0.4 fusion.82
  78.9 1.9 %collective-permute-start = (f32[2,128,256]{1,2,0:T(8,128)S(1)}, f32[2,128,256]{1,2,0:T(8,128)S(1)}, u32[]{:S(2)}, u32[]{:S(2)}) collective-permute-start(f32[2,128,256]{1,2,0:T(8,128)S(1)} %get-tuple-element.288), channel_id=1, source_target_pairs={{0,4},{4,8},{8,12},{12,16},{16,20},{20,24},{24,28},{1,5},{5,9},{9,... | collective-permute-start | bytes 786440 | tf_op jit(solution)/shard_map/while/body/eval_jaxpr/ppermute | solution.py:19
  80.8 6.1 %collective-permute-done = f32[2,128,256]{1,2,0:T(8,128)S(1)} collective-permute-done((f32[2,128,256]{1,2,0:T(8,128)S(1)}, f32[2,128,256]{1,2,0:T(8,128)S(1)}, u32[]{:S(2)}, u32[]{:S(2)}) %collective-permute-start) | collective-permute-done | bytes 262176 | tf_op jit(solution)/shard_map/while/body/eval_jaxpr/ppermute | solution.py:19
  87.1 0.2 fusion.79
  87.4 0.3 fusion.83
  87.8 0.4 fusion.82
  88.2 1.9 %collective-permute-start = (f32[2,128,256]{1,2,0:T(8,128)S(1)}, f32[2,128,256]{1,2,0:T(8,128)S(1)}, u32[]{:S(2)}, u32[]{:S(2)}) collective-permute-start(f32[2,128,256]{1,2,0:T(8,128)S(1)} %get-tuple-element.288), channel_id=1, source_target_pairs={{0,4},{4,8},{8,12},{12,16},{16,20},{20,24},{24,28},{1,5},{5,9},{9,... | collective-permute-start | bytes 786440 | tf_op jit(solution)/shard_map/while/body/eval_jaxpr/ppermute | solution.py:19
  90.2 6.1 %collective-permute-done = f32[2,128,256]{1,2,0:T(8,128)S(1)} collective-permute-done((f32[2,128,256]{1,2,0:T(8,128)S(1)}, f32[2,128,256]{1,2,0:T(8,128)S(1)}, u32[]{:S(2)}, u32[]{:S(2)}) %collective-permute-start) | collective-permute-done | bytes 262176 | tf_op jit(solution)/shard_map/while/body/eval_jaxpr/ppermute | solution.py:19
  96.4 0.2 fusion.79
  96.8 0.3 fusion.83
  97.1 0.4 fusion.82
  97.6 1.9 %collective-permute-start = (f32[2,128,256]{1,2,0:T(8,128)S(1)}, f32[2,128,256]{1,2,0:T(8,128)S(1)}, u32[]{:S(2)}, u32[]{:S(2)}) collective-permute-start(f32[2,128,256]{1,2,0:T(8,128)S(1)} %get-tuple-element.288), channel_id=1, source_target_pairs={{0,4},{4,8},{8,12},{12,16},{16,20},{20,24},{24,28},{1,5},{5,9},{9,... | collective-permute-start | bytes 786440 | tf_op jit(solution)/shard_map/while/body/eval_jaxpr/ppermute | solution.py:19
  99.5 6.1 %collective-permute-done = f32[2,128,256]{1,2,0:T(8,128)S(1)} collective-permute-done((f32[2,128,256]{1,2,0:T(8,128)S(1)}, f32[2,128,256]{1,2,0:T(8,128)S(1)}, u32[]{:S(2)}, u32[]{:S(2)}) %collective-permute-start) | collective-permute-done | bytes 262176 | tf_op jit(solution)/shard_map/while/body/eval_jaxpr/ppermute | solution.py:19
  105.7 0.2 fusion.79
  106.1 0.3 fusion.83
  106.4 0.4 fusion.82
  106.9 0.2 copy.145
  107.1 3.7 %convolution_convert_fusion = bf16[128,2048]{1,0:T(8,128)(2,1)} fusion(bf16[128,1024]{0,1:T(8,128)(2,1)S(1)} %bitcast.152, bf16[1024,2048]{1,0:T(8,128)(2,1)} %param.15), kind=kOutput, calls=%fused_computation.17 | convolution fusion | flops 537133056 | bytes 4980736 | tf_op jit(solution)/shard_map/dot_general | solution.py:143
  110.9 16.5 %reduce-scatter.2.cloned.1.call-done = bf16[128,1024]{1,0:T(8,128)(2,1)} async-done(((bf16[128,2048]{1,0:T(8,128)(2,1)}), bf16[128,1024]{1,0:T(8,128)(2,1)}) %reduce-scatter.2.cloned.1.call-update) | async-done | bytes 262160 | tf_op jit(solution)/shard_map/reduce_scatter | solution.py:144
  (67 shorter events, 2.2 us)
Async XLA Ops:
  6.5 120.8 %reduce-scatter.2.cloned.1.call-start = ((), (), s32[]{:S(2)}) async-start(), calls=%async_computation.1 | async-start | bytes 786432 | tf_op jit(solution)/shard_map/reduce_scatter | solution.py:144
  38.6 10.0 %collective-permute-start = (f32[2,128,256]{1,2,0:T(8,128)S(1)}, f32[2,128,256]{1,2,0:T(8,128)S(1)}, u32[]{:S(2)}, u32[]{:S(2)}) collective-permute-start(f32[2,128,256]{1,2,0:T(8,128)S(1)} %get-tuple-element.288), channel_id=1, source_target_pairs={{0,4},{4,8},{8,12},{12,16},{16,20},{20,24},{24,28},{1,5},{5,9},{9,... | collective-permute-start | bytes 786440 | tf_op jit(solution)/shard_map/while/body/eval_jaxpr/ppermute | solution.py:19
  49.9 9.0 %collective-permute-start = (f32[2,128,256]{1,2,0:T(8,128)S(1)}, f32[2,128,256]{1,2,0:T(8,128)S(1)}, u32[]{:S(2)}, u32[]{:S(2)}) collective-permute-start(f32[2,128,256]{1,2,0:T(8,128)S(1)} %get-tuple-element.288), channel_id=1, source_target_pairs={{0,4},{4,8},{8,12},{12,16},{16,20},{20,24},{24,28},{1,5},{5,9},{9,... | collective-permute-start | bytes 786440 | tf_op jit(solution)/shard_map/while/body/eval_jaxpr/ppermute | solution.py:19
  60.2 8.0 %collective-permute-start = (f32[2,128,256]{1,2,0:T(8,128)S(1)}, f32[2,128,256]{1,2,0:T(8,128)S(1)}, u32[]{:S(2)}, u32[]{:S(2)}) collective-permute-start(f32[2,128,256]{1,2,0:T(8,128)S(1)} %get-tuple-element.288), channel_id=1, source_target_pairs={{0,4},{4,8},{8,12},{12,16},{16,20},{20,24},{24,28},{1,5},{5,9},{9,... | collective-permute-start | bytes 786440 | tf_op jit(solution)/shard_map/while/body/eval_jaxpr/ppermute | solution.py:19
  69.6 8.0 %collective-permute-start = (f32[2,128,256]{1,2,0:T(8,128)S(1)}, f32[2,128,256]{1,2,0:T(8,128)S(1)}, u32[]{:S(2)}, u32[]{:S(2)}) collective-permute-start(f32[2,128,256]{1,2,0:T(8,128)S(1)} %get-tuple-element.288), channel_id=1, source_target_pairs={{0,4},{4,8},{8,12},{12,16},{16,20},{20,24},{24,28},{1,5},{5,9},{9,... | collective-permute-start | bytes 786440 | tf_op jit(solution)/shard_map/while/body/eval_jaxpr/ppermute | solution.py:19
  78.9 8.0 %collective-permute-start = (f32[2,128,256]{1,2,0:T(8,128)S(1)}, f32[2,128,256]{1,2,0:T(8,128)S(1)}, u32[]{:S(2)}, u32[]{:S(2)}) collective-permute-start(f32[2,128,256]{1,2,0:T(8,128)S(1)} %get-tuple-element.288), channel_id=1, source_target_pairs={{0,4},{4,8},{8,12},{12,16},{16,20},{20,24},{24,28},{1,5},{5,9},{9,... | collective-permute-start | bytes 786440 | tf_op jit(solution)/shard_map/while/body/eval_jaxpr/ppermute | solution.py:19
  88.2 8.0 %collective-permute-start = (f32[2,128,256]{1,2,0:T(8,128)S(1)}, f32[2,128,256]{1,2,0:T(8,128)S(1)}, u32[]{:S(2)}, u32[]{:S(2)}) collective-permute-start(f32[2,128,256]{1,2,0:T(8,128)S(1)} %get-tuple-element.288), channel_id=1, source_target_pairs={{0,4},{4,8},{8,12},{12,16},{16,20},{20,24},{24,28},{1,5},{5,9},{9,... | collective-permute-start | bytes 786440 | tf_op jit(solution)/shard_map/while/body/eval_jaxpr/ppermute | solution.py:19
  97.6 8.0 %collective-permute-start = (f32[2,128,256]{1,2,0:T(8,128)S(1)}, f32[2,128,256]{1,2,0:T(8,128)S(1)}, u32[]{:S(2)}, u32[]{:S(2)}) collective-permute-start(f32[2,128,256]{1,2,0:T(8,128)S(1)} %get-tuple-element.288), channel_id=1, source_target_pairs={{0,4},{4,8},{8,12},{12,16},{16,20},{20,24},{24,28},{1,5},{5,9},{9,... | collective-permute-start | bytes 786440 | tf_op jit(solution)/shard_map/while/body/eval_jaxpr/ppermute | solution.py:19
Sparse Core Ops, SparseCore 0:
  111.0 16.3 reduce-scatter.1
where the time goes:
time: 136 us; the launch traced here: 134 us
  waiting for transfers between devices  60.5 us (44%)
  other arithmetic  21.6 us (16%)
  matrix products  16 us (12%)
  starting transfers between devices  14.9 us (11%)
  between operations  13.6 us (10%)
  local copies, waits for them, and re-layouts  6.93 us (5%)
    ppermute x7, waiting for transfers between devices, shifted(): return lax.ppermute(value, axis, pairs)  44.1 us
    another operation x2, other arithmetic, lower_solve(): lax.linalg.triangular_solve(matrix, right, left_side=True, lower=True)  19.7 us
    reduce_scatter x1, waiting for transfers between devices, per_device(): lax.psum_scatter(partial_out.astype(jnp.bfloat16), 'heads', scatter_dimen...  16.5 us
    ppermute x7, starting transfers between devices, shifted(): return lax.ppermute(value, axis, pairs)  14.9 us
    unnamed x5, local copies, waits for them, and re-layouts  4.09 us
    dot_general x1, matrix products, per_device(): jnp.dot(attended, out_weight, preferred_element_type=jnp.float32)  3.72 us
    dot_general x7, matrix products, absorb(): jnp.einsum('tgqj,jgd->tgqd', far_weights.astype(jnp.bfloat16), far_values...  3.15 us
  transfers between devices with their start and end apart: 8, of which 8 were waited for; matrix products, arithmetic and copies ran while one was open for 0% of the time, Pallas kernels for 0%

commit v1 on v0

v1 whole, which is shorter than its diff:
```python
import functools
import math

import jax
import jax.numpy as jnp
from jax import lax
from jax.experimental import pallas as pl
from jax.experimental.pallas import tpu as pltpu
from jax.sharding import PartitionSpec as P

HD = 128
norm_floor = 1e-06
masked_score = -1e30
MESH = pl.DeviceIdType.MESH
f32 = jnp.float32
bf16 = jnp.bfloat16


def split(a):
    hi = a.astype(bf16)
    return hi, (a - hi.astype(f32)).astype(bf16)


def dot(a, b):
    return jnp.dot(a, b, preferred_element_type=f32)


def dot_two(ah, al, b):
    return dot(jnp.concatenate([ah, al], 1), jnp.concatenate([b, b], 0))


def dot_three(ah, al, bh, bl):
    return dot_two(ah, al, bh) + dot(ah, bl)


def kernel(n, cols, peers, groups, per_group, chunks, *refs):
    (q_ref, k_ref, v_ref, h_ref, beta_ref, w_hbm, o_ref,
     w_ref, own, far, vals, turned_ref, prod_ref, max_ref, sum_ref, acc_ref,
     part_out, part_in,
     w_sem, v_send, v_send_row, v_rel, v_recv, e_send, e_send_row, e_rel, e_recv,
     p_send, p_recv) = refs
    rows = n // cols
    tok = q_ref.shape[0]
    me = lax.axis_index("seq")
    head = lax.axis_index("heads")
    z = lax.div(me, cols)
    x = lax.rem(me, cols)

    def copy_w(j):
        width = w_ref.shape[1] // peers
        at = pl.ds(j * width, width)
        return pltpu.make_async_copy(w_hbm.at[:, at], w_ref.at[:, at], w_sem.at[j])

    for j in range(peers):
        copy_w(j).start()

    barrier = pltpu.get_barrier_semaphore()
    for dz in range(1, rows):
        there = lax.rem(z + dz, rows) * cols + x
        pl.semaphore_signal(barrier, inc=1, device_id={"seq": there}, device_id_type=MESH)
    for dx in range(1, cols):
        there = z * cols + lax.rem(x + dx, cols)
        pl.semaphore_signal(barrier, inc=1, device_id={"seq": there}, device_id_type=MESH)
    for dh in range(1, peers):
        there = lax.rem(head + dh, peers)
        pl.semaphore_signal(barrier, inc=1, device_id={"heads": there}, device_id_type=MESH)
    pl.semaphore_wait(barrier, rows + cols + peers - 3)

    def column_copy(source, slots, send, recv, z2):
        return pltpu.make_async_remote_copy(
            src_ref=source, dst_ref=slots.at[me], send_sem=send.at[z2], recv_sem=recv.at[me],
            device_id={"seq": z2 * cols + x}, device_id_type=MESH)

    def row_copy(source, slots, send, recv, x2):
        return pltpu.make_async_remote_copy(
            src_ref=source, dst_ref=slots.at[me], send_sem=send.at[x2], recv_sem=recv.at[me],
            device_id={"seq": z * cols + x2}, device_id_type=MESH)

    def relay_copy(slots, send, recv, zr, dx):
        block = zr * cols + x
        return pltpu.make_async_remote_copy(
            src_ref=slots.at[block], dst_ref=slots.at[block], send_sem=send.at[zr, dx],
            recv_sem=recv.at[block],
            device_id={"seq": z * cols + lax.rem(x + dx, cols)}, device_id_type=MESH)

    def wait_block(slots, recv, block):
        pltpu.make_async_remote_copy(
            src_ref=slots.at[block], dst_ref=slots.at[block], send_sem=w_sem.at[0],
            recv_sem=recv.at[block], device_id={"heads": lax.rem(head + 1, peers)},
            device_id_type=MESH).wait_recv()

    def loop(lower, upper, body):
        def step(i, carry):
            body(i)
            return carry
        lax.fori_loop(lower, upper, step, 0)

    def send_all(source, slots, send, send_row, recv):
        loop(x + 1, cols, lambda x2: row_copy(source, slots, send_row, recv, x2).start())
        loop(z + 1, rows, lambda z2: column_copy(source, slots, send, recv, z2).start())

    def sent_all(source, slots, send, send_row, rel, recv):
        loop(x + 1, cols, lambda x2: row_copy(source, slots, send_row, recv, x2).wait_send())
        loop(z + 1, rows, lambda z2: column_copy(source, slots, send, recv, z2).wait_send())

        def one(zr):
            for dx in range(1, cols):
                relay_copy(slots, rel, recv, zr, dx).wait_send()
        loop(0, z, one)

    def relay(slots, rel, recv, zr):
        wait_block(slots, recv, zr * cols + x)
        for dx in range(1, cols):
            relay_copy(slots, rel, recv, zr, dx).start()

    send_all(v_ref, vals, v_send, v_send_row, v_recv)

    row = lax.broadcasted_iota(jnp.int32, (tok, tok), 0)
    col = lax.broadcasted_iota(jnp.int32, (tok, tok), 1)
    diag = row == col
    eye = diag.astype(f32)
    below = col < row
    differ = row ^ col
    upto = jnp.concatenate([col <= row] * per_group, 0)
    scale = math.log2(math.e) / math.sqrt(HD)
    span = range(groups)

    def lanes(g):
        return slice(g * HD, (g + 1) * HD)

    h = [h_ref[:, lanes(g)] for g in span]
    k = [k_ref[:, lanes(g)] for g in span]
    q = [jnp.concatenate([q_ref[:, lanes(g * per_group + i)] for i in range(per_group)], 0)
         for g in span]
    h_t = [h[g].T for g in span]
    k_t = [k[g].T for g in span]
    hk_t = [jnp.concatenate([h_t[g], k_t[g]], 1) for g in span]
    first = [dot(h[g], hk_t[g]) for g in span]
    gram = [first[g][:, :tok] for g in span]
    square = [jnp.where(diag, gram[g], 0.0) for g in span]
    s_col = [lax.rsqrt(jnp.sum(square[g], 1, keepdims=True) + norm_floor) for g in span]
    s_row = [lax.rsqrt(jnp.sum(square[g], 0, keepdims=True) + norm_floor) for g in span]
    beta_row = [beta_ref[g:g + 1, :] for g in span]
    beta_col = [jnp.sum(jnp.where(diag, beta_row[g], 0.0), 1, keepdims=True) for g in span]
    strict = [jnp.where(below, gram[g] * (s_col[g] * beta_col[g]) * s_row[g], 0.0) for g in span]
    key_along = [jnp.where(below, first[g][:, tok:] * s_col[g], 0.0) for g in span]
    parts = [split(strict[g]) for g in span]
    inverse = [eye - jnp.where(differ == 1, strict[g], 0.0) for g in span]
    size = 2
    while size < tok:
        mask = (differ >= size) & (differ < 2 * size)
        halves = [split(inverse[g]) for g in span]
        zero = jnp.zeros((tok, tok), bf16)
        inner = [dot_three(jnp.where(mask, parts[g][0], zero), jnp.where(mask, parts[g][1], zero),
                           *halves[g]) for g in span]
        inner = [split(inner[g]) for g in span]
        inverse = [inverse[g] - dot_three(*halves[g], *inner[g]) for g in span]
        size *= 2
    solver = [split(inverse[g] * beta_row[g]) for g in span]
    right = [split(jnp.concatenate([h[g].astype(f32) * s_col[g], key_along[g]], 1)) for g in span]
    solved = [dot_three(*solver[g], *right[g]) for g in span]
    scaled = [split(solved[g] * s_col[g]) for g in span]
    for g in span:
        base = jnp.concatenate([eye, k_t[g].astype(f32)], 1)
        turn = dot(jnp.concatenate([h_t[g], h_t[g]], 1), jnp.concatenate(scaled[g], 0))
        own[g * HD:(g + 1) * HD, :] = (base - turn).astype(bf16)
    send_all(own, far, e_send, e_send_row, e_recv)

    for g in span:
        second = dot(q[g], hk_t[g])
        along = split(jnp.where(upto, second[:, :tok] * s_row[g], 0.0))
        base = jnp.concatenate([q[g].astype(f32), second[:, tok:]], 1)
        both = base - dot_three(*along, *split(solved[g]))
        turned_ref[g] = both[:, :HD].astype(bf16)
        score = jnp.where(upto, both[:, HD:] * scale, masked_score)
        top = jnp.max(score, 1, keepdims=True)
        expo = jnp.exp2(score - top)
        max_ref[g] = jnp.broadcast_to(top, max_ref.shape[1:])
        sum_ref[g] = expo
        acc_ref[g] = dot(expo.astype(bf16), v_ref[:, lanes(g)])
        prod_ref[g] = eye

    loop(0, z, lambda i: relay(vals, v_rel, v_recv, z - 1 - i))

    def absorb(i):
        block = me - 1 - i
        zr = lax.div(block, cols)
        xr = lax.rem(block, cols)
        earlier = zr < z

        @pl.when(earlier & (xr == cols - 1))
        def _():
            relay(far, e_rel, e_recv, zr)

        @pl.when(jnp.logical_not(earlier & (xr == x)))
        def _():
            wait_block(vals, v_recv, block)
            wait_block(far, e_recv, block)

        for g in span:
            moved = dot_two(*split(prod_ref[g]), far[block, g * HD:(g + 1) * HD, :])
            prod_ref[g] = moved[:, :HD]
            score = dot(turned_ref[g], moved[:, HD:].astype(bf16)) * scale
            old = max_ref[g]
            top = jnp.maximum(old, jnp.max(score, 1, keepdims=True))
            shrink = jnp.exp2(old - top)
            expo = jnp.exp2(score - top)
            max_ref[g] = top
            sum_ref[g] = sum_ref[g] * shrink + expo
            acc_ref[g] = acc_ref[g] * shrink + dot(expo.astype(bf16), vals[block, :, lanes(g)])

    loop(0, me, absorb)

    pieces = []
    for g in span:
        total = jnp.sum(sum_ref[g], 1, keepdims=True)
        mean = (acc_ref[g] / total).astype(bf16)
        pieces += [mean[i * tok:(i + 1) * tok] for i in range(per_group)]
    attended = jnp.concatenate(pieces, 1)
    width = o_ref.shape[1]
    part = width // chunks

    def part_copy(dh, c):
        at = pl.ds(c * part, part)
        return pltpu.make_async_remote_copy(
            src_ref=part_out.at[dh - 1, :, at], dst_ref=part_in.at[dh - 1, :, at],
            send_sem=p_send.at[dh - 1, c], recv_sem=p_recv.at[dh - 1, c],
            device_id={"heads": lax.rem(head + dh, peers)}, device_id_type=MESH)

    for j in range(peers):
        copy_w(j).wait()
    for dh in range(1, peers):
        there = lax.rem(head + dh, peers)
        for c in range(chunks):
            at = pl.ds(pl.multiple_of(there * width + c * part, part), part)
            part_out[dh - 1, :, c * part:(c + 1) * part] = dot(attended, w_ref[:, at]).astype(bf16)
            part_copy(dh, c).start()
    mine = []
    for c in range(chunks):
        at = pl.ds(pl.multiple_of(head * width + c * part, part), part)
        mine.append(dot(attended, w_ref[:, at]))
    for c in range(chunks):
        total = mine[c]
        for dh in range(1, peers):
            part_copy(dh, c).wait_recv()
            total = total + part_in[dh - 1, :, c * part:(c + 1) * part].astype(f32)
        o_ref[:, c * part:(c + 1) * part] = total.astype(o_ref.dtype)

    sent_all(v_ref, vals, v_send, v_send_row, v_rel, v_recv)
    sent_all(own, far, e_send, e_send_row, e_rel, e_recv)
    for dh in range(1, peers):
        for c in range(chunks):
            part_copy(dh, c).wait_send()


def per_device(n, peers, queries, keys, values, house, beta, out_weight):
    tok = queries.shape[0]
    groups = keys.shape[1] // HD
    per_group = queries.shape[1] // keys.shape[1]
    width = out_weight.shape[1] // peers
    cols = max(c for c in range(1, n + 1) if n % c == 0 and c * c <= n)
    rows = n // cols
    chunks = 2
    many = per_group * tok
    vmem = pl.BlockSpec(memory_space=pltpu.VMEM)
    dma = pltpu.SemaphoreType.DMA
    body = functools.partial(kernel, n, cols, peers, groups, per_group, chunks)
    return pl.pallas_call(
        body,
        out_shape=jax.ShapeDtypeStruct((tok, width), bf16),
        in_specs=[vmem] * 5 + [pl.BlockSpec(memory_space=pl.ANY)],
        out_specs=vmem,
        scratch_shapes=[
            pltpu.VMEM(out_weight.shape, bf16),
            pltpu.VMEM((groups * HD, HD + tok), bf16),
            pltpu.VMEM((n, groups * HD, HD + tok), bf16),
            pltpu.VMEM((n,) + values.shape, bf16),
            pltpu.VMEM((groups, many, HD), bf16),
            pltpu.VMEM((groups, HD, HD), f32),
            pltpu.VMEM((groups, many, tok), f32),
            pltpu.VMEM((groups, many, tok), f32),
            pltpu.VMEM((groups, many, HD), f32),
            pltpu.VMEM((peers - 1, tok, width), bf16),
            pltpu.VMEM((peers - 1, tok, width), bf16),
            dma((peers,)),
            dma((rows,)), dma((cols,)), dma((rows, cols)), dma((n,)),
            dma((rows,)), dma((cols,)), dma((rows, cols)), dma((n,)),
            dma((peers - 1, chunks)), dma((peers - 1, chunks)),
        ],
        compiler_params=pltpu.CompilerParams(
            collective_id=0, has_side_effects=True, vmem_limit_bytes=48 * 2**20
        ),
    )(queries, keys, values, house, beta, out_weight)


def solution(mesh):
    in_specs = (
        P(("dp", "seq"), "heads"),
        P(("dp", "seq"), "heads"),
        P(("dp", "seq"), "heads"),
        P(("dp", "seq"), "heads"),
        P("heads", ("dp", "seq")),
        P("heads", None),
    )
    out_specs = P(("dp", "seq"), "heads")
    body = functools.partial(per_device, mesh.shape["seq"], mesh.shape["heads"])
    return jax.shard_map(
        body, mesh=mesh, in_specs=in_specs, out_specs=out_specs, check_vma=False
    )
```

time: 136 us -> 41.7 us (0.31); the launches traced: 134 us -> 41.4 us
  waiting for transfers between devices: 60.5 us -> 0 us
  Pallas kernels: 0 us -> 34.3 us
  other arithmetic: 21.6 us -> 0 us
  matrix products: 16 us -> 0 us
  starting transfers between devices: 14.9 us -> 0 us
  between operations: 13.6 us -> 0.02 us
    ppermute x7 -> x0, waiting for transfers between devices: 44.1 us -> none  [shifted(): return lax.ppermute(value, axis, pairs)]
    pallas_call x0 -> x1, Pallas kernels: none -> 34.3 us  [per_device(): pl.pallas_call(body, out_shape=jax.ShapeDtypeStruct((tok, width), bf16),...]
    another operation x10 -> x0, other arithmetic: 19.8 us -> none  [the longest x2 19.7 us: lower_solve(): lax.linalg.triangular_solve(matrix, right, left_side=True, lower=True)]
    reduce_scatter x1 -> x0, waiting for transfers between devices: 16.5 us -> none  [per_device(): lax.psum_scatter(partial_out.astype(jnp.bfloat16), 'heads', scatter_dimen...]
    ppermute x7 -> x0, starting transfers between devices: 14.9 us -> none  [shifted(): return lax.ppermute(value, axis, pairs)]
    dot_general x31 -> x0, matrix products: 14.6 us -> none  [the longest x1 3.72 us: per_device(): jnp.dot(attended, out_weight, preferred_element_type=jnp.float32)]
    unnamed x5 -> x13, local copies, waits for them, and re-layouts: 4.09 us -> 7.04 us
    another operation x3 -> x0, matrix products: 1.42 us -> none  [the longest x2 0.83 us: lower_solve(): lax.linalg.triangular_solve(matrix, right, left_side=True, lower=True)]
  transfers between devices with their start and end apart: 8 -> 0, of which waited for: 8 -> 0; matrix products, arithmetic and copies ran while one was open for 0% -> 0% of each run, Pallas kernels for 0% -> 0%
where the time goes in v1:
time: 41.7 us; the launch traced here: 41.4 us
  Pallas kernels  34.3 us (82%)
  local copies, waits for them, and re-layouts  7.04 us (17%)
    pallas_call x1, Pallas kernels, per_device(): pl.pallas_call(body, out_shape=jax.ShapeDtypeStruct((tok, width), bf16),...  34.3 us
    unnamed x13, local copies, waits for them, and re-layouts  7.04 us

profile of v1, /device:TPU:25, one launch (start us, length us, event | category | flops | bytes accessed | tf_op | source)
XLA Modules:
  0.0 41.4 jit_solution(9029310400066093793)
XLA Ops:
  0.0 0.0 copy-start
  0.0 2.2 %copy-done = bf16[1024,2048]{1,0:T(8,128)(2,1)S(1)} copy-done((bf16[1024,2048]{1,0:T(8,128)(2,1)S(1)}, bf16[1024,2048]{1,0:T(8,128)(2,1)}, u32[]{:S(2)}) %copy-start) | copy-done | bytes 4194328
  2.2 0.0 copy-start.1
  2.2 0.9 %copy-done.1 = bf16[128,1024]{1,0:T(8,128)(2,1)S(1)} copy-done((bf16[128,1024]{1,0:T(8,128)(2,1)S(1)}, bf16[128,1024]{1,0:T(8,128)(2,1)}, u32[]{:S(2)}) %copy-start.1) | copy-done | bytes 262168
  3.1 0.0 copy-start.2
  3.1 0.8 %copy-done.2 = bf16[128,256]{1,0:T(8,128)(2,1)S(1)} copy-done((bf16[128,256]{1,0:T(8,128)(2,1)S(1)}, bf16[128,256]{1,0:T(8,128)(2,1)}, u32[]{:S(2)}) %copy-start.2) | copy-done | bytes 65560
  4.0 0.0 copy-start.3
  4.0 0.8 %copy-done.3 = bf16[128,256]{1,0:T(8,128)(2,1)S(1)} copy-done((bf16[128,256]{1,0:T(8,128)(2,1)S(1)}, bf16[128,256]{1,0:T(8,128)(2,1)}, u32[]{:S(2)}) %copy-start.3) | copy-done | bytes 65560
  4.8 0.0 copy-start.4
  4.8 0.8 %copy-done.4 = bf16[128,256]{1,0:T(8,128)(2,1)S(1)} copy-done((bf16[128,256]{1,0:T(8,128)(2,1)S(1)}, bf16[128,256]{1,0:T(8,128)(2,1)}, u32[]{:S(2)}) %copy-start.4) | copy-done | bytes 65560
  5.7 0.0 copy-start.5
  5.7 0.7 %copy-done.5 = f32[2,128]{1,0:T(2,128)S(1)} copy-done((f32[2,128]{1,0:T(2,128)S(1)}, f32[2,128]{1,0:T(2,128)}, u32[]{:S(2)}) %copy-start.5) | copy-done | bytes 1048
  6.3 34.3 %shard_map.64 = bf16[128,1024]{1,0:T(8,128)(2,1)S(1)} custom-call(bf16[128,1024]{1,0:T(8,128)(2,1)S(1)} %copy-done.1, bf16[128,256]{1,0:T(8,128)(2,1)S(1)} %copy-done.2, bf16[128,256]{1,0:T(8,128)(2,1)S(1)} %copy-done.3, bf16[128,256]{1,0:T(8,128)(2,1)S(1)} %copy-done.4, f32[2,128]{1,0:T(2,128)S(1)} %copy-done.5, bf16[1024,2048]{1,0:T(8,128)(2,1)S(1)} %copy-done), custom_call_target="tpu_custom_call" | custom-call | tf_op jit(solution)/shard_map/pallas_call | solution.py:268
  40.7 0.7 %copy.8 = bf16[128,1024]{1,0:T(8,128)(2,1)} copy(bf16[128,1024]{1,0:T(8,128)(2,1)S(1)} %shard_map.64) | data formatting | bytes 524288
Async XLA Ops:
  0.0 2.2 %copy-start = (bf16[1024,2048]{1,0:T(8,128)(2,1)S(1)}, bf16[1024,2048]{1,0:T(8,128)(2,1)}, u32[]{:S(2)}) copy-start(bf16[1024,2048]{1,0:T(8,128)(2,1)} %refs_5_.1) | copy-start | bytes 12582916
  2.2 0.9 %copy-start.1 = (bf16[128,1024]{1,0:T(8,128)(2,1)S(1)}, bf16[128,1024]{1,0:T(8,128)(2,1)}, u32[]{:S(2)}) copy-start(bf16[128,1024]{1,0:T(8,128)(2,1)} %refs_0_.1) | copy-start | bytes 786436
  3.1 0.8 %copy-start.2 = (bf16[128,256]{1,0:T(8,128)(2,1)S(1)}, bf16[128,256]{1,0:T(8,128)(2,1)}, u32[]{:S(2)}) copy-start(bf16[128,256]{1,0:T(8,128)(2,1)} %refs_1_.1) | copy-start | bytes 196612
  4.0 0.8 %copy-start.3 = (bf16[128,256]{1,0:T(8,128)(2,1)S(1)}, bf16[128,256]{1,0:T(8,128)(2,1)}, u32[]{:S(2)}) copy-start(bf16[128,256]{1,0:T(8,128)(2,1)} %refs_2_.1) | copy-start | bytes 196612
  4.8 0.8 %copy-start.4 = (bf16[128,256]{1,0:T(8,128)(2,1)S(1)}, bf16[128,256]{1,0:T(8,128)(2,1)}, u32[]{:S(2)}) copy-start(bf16[128,256]{1,0:T(8,128)(2,1)} %refs_3_.1) | copy-start | bytes 196612
  5.7 0.7 %copy-start.5 = (f32[2,128]{1,0:T(2,128)S(1)}, f32[2,128]{1,0:T(2,128)}, u32[]{:S(2)}) copy-start(f32[2,128]{1,0:T(2,128)} %refs_4_.1) | copy-start | bytes 3076

commit v2 on v1

--- a/solution.py
+++ b/solution.py
@@ -34,11 +34,11 @@
 
 
 def kernel(n, cols, peers, groups, per_group, chunks, *refs):
-    (q_ref, k_ref, v_ref, h_ref, beta_ref, w_hbm, o_ref,
-     w_ref, own, far, vals, turned_ref, prod_ref, max_ref, sum_ref, acc_ref,
-     part_out, part_in,
-     w_sem, v_send, v_send_row, v_rel, v_recv, e_send, e_send_row, e_rel, e_recv,
-     p_send, p_recv) = refs
+    (q_hbm, k_hbm, v_hbm, h_hbm, beta_hbm, w_hbm, o_ref,
+     q_ref, k_ref, v_ref, h_ref, beta_ref, w_ref, ends, maps, far, passed, vals,
+     turned_ref, prod_ref, row_map, max_ref, sum_ref, acc_ref, part_out, part_in,
+     in_sem, w_sem, v_send, v_send_row, v_rel, v_recv, m_send, m_recv,
+     e_send, e_send_row, e_rel, e_recv, p_send, p_recv) = refs
     rows = n // cols
     tok = q_ref.shape[0]
     me = lax.axis_index("seq")
@@ -46,6 +46,12 @@
     z = lax.div(me, cols)
     x = lax.rem(me, cols)
 
+    small = [pltpu.make_async_copy(source, target, in_sem.at[i]) for i, (source, target) in
+             enumerate([(v_hbm, v_ref), (h_hbm, h_ref), (k_hbm, k_ref), (beta_hbm, beta_ref),
+                        (q_hbm, q_ref)])]
+    for copy in small:
+        copy.start()
+
     def copy_w(j):
         width = w_ref.shape[1] // peers
         at = pl.ds(j * width, width)
@@ -55,7 +61,7 @@
         copy_w(j).start()
 
     barrier = pltpu.get_barrier_semaphore()
-    for dz in range(1, rows):
+    for dz in (1, rows - 1):
         there = lax.rem(z + dz, rows) * cols + x
         pl.semaphore_signal(barrier, inc=1, device_id={"seq": there}, device_id_type=MESH)
     for dx in range(1, cols):
@@ -64,16 +70,17 @@
     for dh in range(1, peers):
         there = lax.rem(head + dh, peers)
         pl.semaphore_signal(barrier, inc=1, device_id={"heads": there}, device_id_type=MESH)
-    pl.semaphore_wait(barrier, rows + cols + peers - 3)
-
-    def column_copy(source, slots, send, recv, z2):
+    pl.semaphore_wait(barrier, cols + peers)
+
+    def to_next(source, slots, send, recv, zr):
         return pltpu.make_async_remote_copy(
-            src_ref=source, dst_ref=slots.at[me], send_sem=send.at[z2], recv_sem=recv.at[me],
-            device_id={"seq": z2 * cols + x}, device_id_type=MESH)
-
-    def row_copy(source, slots, send, recv, x2):
+            src_ref=source, dst_ref=slots.at[zr * cols + x], send_sem=send.at[zr],
+            recv_sem=recv.at[zr * cols + x],
+            device_id={"seq": lax.rem(z + 1, rows) * cols + x}, device_id_type=MESH)
+
+    def row_copy(source, slots, send, recv, x2, at):
         return pltpu.make_async_remote_copy(
-            src_ref=source, dst_ref=slots.at[me], send_sem=send.at[x2], recv_sem=recv.at[me],
+            src_ref=source, dst_ref=slots.at[at], send_sem=send.at[x2], recv_sem=recv.at[at],
             device_id={"seq": z * cols + x2}, device_id_type=MESH)
 
     def relay_copy(slots, send, recv, zr, dx):
@@ -95,25 +102,35 @@
             return carry
         lax.fori_loop(lower, upper, step, 0)
 
-    def send_all(source, slots, send, send_row, recv):
-        loop(x + 1, cols, lambda x2: row_copy(source, slots, send_row, recv, x2).start())
-        loop(z + 1, rows, lambda z2: column_copy(source, slots, send, recv, z2).start())
-
-    def sent_all(source, slots, send, send_row, rel, recv):
-        loop(x + 1, cols, lambda x2: row_copy(source, slots, send_row, recv, x2).wait_send())
-        loop(z + 1, rows, lambda z2: column_copy(source, slots, send, recv, z2).wait_send())
-
-        def one(zr):
-            for dx in range(1, cols):
-                relay_copy(slots, rel, recv, zr, dx).wait_send()
-        loop(0, z, one)
-
-    def relay(slots, rel, recv, zr):
-        wait_block(slots, recv, zr * cols + x)
+    more = z + 1 < rows
+
+    def row_maps(body):
         for dx in range(1, cols):
-            relay_copy(slots, rel, recv, zr, dx).start()
-
-    send_all(v_ref, vals, v_send, v_send_row, v_recv)
+            body(row_copy(maps.at[x], maps, m_send, m_recv, lax.rem(x + dx, cols), x))
+
+    def relay_values(zr):
+        wait_block(vals, v_recv, zr * cols + x)
+
+        @pl.when(more)
+        def _():
+            to_next(vals.at[zr * cols + x], vals, v_send, v_recv, zr).start()
+        for dx in range(1, cols):
+            relay_copy(vals, v_rel, v_recv, zr, dx).start()
+
+    def relay_values_at(step):
+        @pl.when(z - step >= 0)
+        def _():
+            relay_values(z - step)
+
+    small[0].wait()
+
+    @pl.when(more)
+    def _():
+        to_next(v_ref, vals, v_send, v_recv, z).start()
+    loop(x + 1, cols,
+         lambda x2: row_copy(v_ref, vals, v_send_row, v_recv, x2, me).start())
+    for copy in small[1:]:
+        copy.wait()
 
     row = lax.broadcasted_iota(jnp.int32, (tok, tok), 0)
     col = lax.broadcasted_iota(jnp.int32, (tok, tok), 1)
@@ -147,6 +164,7 @@
     parts = [split(strict[g]) for g in span]
     inverse = [eye - jnp.where(differ == 1, strict[g], 0.0) for g in span]
     size = 2
+    stage = 0
     while size < tok:
         mask = (differ >= size) & (differ < 2 * size)
         halves = [split(inverse[g]) for g in span]
@@ -155,6 +173,9 @@
                            *halves[g]) for g in span]
         inner = [split(inner[g]) for g in span]
         inverse = [inverse[g] - dot_three(*halves[g], *inner[g]) for g in span]
+        if size in (tok // 16, tok // 4):
+            stage += 1
+            relay_values_at(stage)
         size *= 2
     solver = [split(inverse[g] * beta_row[g]) for g in span]
     right = [split(jnp.concatenate([h[g].astype(f32) * s_col[g], key_along[g]], 1)) for g in span]
@@ -163,10 +184,18 @@
     for g in span:
         base = jnp.concatenate([eye, k_t[g].astype(f32)], 1)
         turn = dot(jnp.concatenate([h_t[g], h_t[g]], 1), jnp.concatenate(scaled[g], 0))
-        own[g * HD:(g + 1) * HD, :] = (base - turn).astype(bf16)
-    send_all(own, far, e_send, e_send_row, e_recv)
-
-    for g in span:
+        made = (base - turn).astype(bf16)
+        maps[x, g * HD:(g + 1) * HD, :] = made[:, :HD]
+        ends[g * HD:(g + 1) * HD, :] = made[:, HD:]
+    row_maps(lambda copy: copy.start())
+
+    @pl.when(more & (x == cols - 1))
+    def _():
+        to_next(ends, far, e_send, e_recv, z).start()
+    loop(x + 1, cols,
+         lambda x2: row_copy(ends, far, e_send_row, e_recv, x2, me).start())
+
+    def own_scores(g):
         second = dot(q[g], hk_t[g])
         along = split(jnp.where(upto, second[:, :tok] * s_row[g], 0.0))
         base = jnp.concatenate([q[g].astype(f32), second[:, tok:]], 1)
@@ -179,8 +208,52 @@
         sum_ref[g] = expo
         acc_ref[g] = dot(expo.astype(bf16), v_ref[:, lanes(g)])
         prod_ref[g] = eye
-
-    loop(0, z, lambda i: relay(vals, v_rel, v_recv, z - 1 - i))
+        row_map[g] = eye
+
+    def under(g):
+        return slice(g * HD, (g + 1) * HD)
+
+    def map_times(block_map, value):
+        return dot(jnp.concatenate([block_map, block_map], 1), jnp.concatenate(split(value), 0))
+
+    for g in range(0, groups, 2):
+        own_scores(g)
+
+    for dx in range(1, cols):
+        wait_block(maps, m_recv, lax.rem(x + dx, cols))
+
+    @pl.when(more & (x < cols - 1))
+    def _():
+        for g in span:
+            def move(xr, value):
+                return map_times(maps[xr, under(g), :], value)
+            value = lax.fori_loop(x + 1, cols, move, ends[under(g), :].astype(f32))
+            passed[z, under(g), :] = value.astype(bf16)
+        to_next(passed.at[z], far, e_send, e_recv, z).start()
+
+    for g in range(1, groups, 2):
+        own_scores(g)
+    for g in span:
+        value = maps[0, under(g), :].astype(f32)
+        for xr in range(1, cols):
+            value = map_times(maps[xr, under(g), :], value)
+        row_map[g] = value
+
+    for step in range(stage + 1, rows):
+        relay_values_at(step)
+
+    def relay_keys(zr):
+        block = zr * cols + x
+        wait_block(far, e_recv, block)
+        for dx in range(1, cols):
+            relay_copy(far, e_rel, e_recv, zr, dx).start()
+
+        @pl.when(more)
+        def _():
+            for g in span:
+                moved = dot_two(*split(row_map[g]), far[block, under(g), :])
+                passed[zr, under(g), :] = moved.astype(bf16)
+            to_next(passed.at[zr], far, e_send, e_recv, zr).start()
 
     def absorb(i):
         block = me - 1 - i
@@ -190,7 +263,7 @@
 
         @pl.when(earlier & (xr == cols - 1))
         def _():
-            relay(far, e_rel, e_recv, zr)
+            relay_keys(zr)
 
         @pl.when(jnp.logical_not(earlier & (xr == x)))
         def _():
@@ -198,9 +271,8 @@
             wait_block(far, e_recv, block)
 
         for g in span:
-            moved = dot_two(*split(prod_ref[g]), far[block, g * HD:(g + 1) * HD, :])
-            prod_ref[g] = moved[:, :HD]
-            score = dot(turned_ref[g], moved[:, HD:].astype(bf16)) * scale
+            moved = dot_two(*split(prod_ref[g]), far[block, under(g), :])
+            score = dot(turned_ref[g], moved.astype(bf16)) * scale
             old = max_ref[g]
             top = jnp.maximum(old, jnp.max(score, 1, keepdims=True))
             shrink = jnp.exp2(old - top)
@@ -208,6 +280,11 @@
             max_ref[g] = top
             sum_ref[g] = sum_ref[g] * shrink + expo
             acc_ref[g] = acc_ref[g] * shrink + dot(expo.astype(bf16), vals[block, :, lanes(g)])
+
+        @pl.when(jnp.logical_not(earlier))
+        def _():
+            for g in span:
+                prod_ref[g] = dot_two(*split(prod_ref[g]), maps[xr, under(g), :])
 
     loop(0, me, absorb)
 
@@ -246,8 +323,25 @@
             total = total + part_in[dh - 1, :, c * part:(c + 1) * part].astype(f32)
         o_ref[:, c * part:(c + 1) * part] = total.astype(o_ref.dtype)
 
-    sent_all(v_ref, vals, v_send, v_send_row, v_rel, v_recv)
-    sent_all(own, far, e_send, e_send_row, e_rel, e_recv)
+    row_maps(lambda copy: copy.wait_send())
+    loop(x + 1, cols,
+         lambda x2: row_copy(v_ref, vals, v_send_row, v_recv, x2, me).wait_send())
+    loop(x + 1, cols,
+         lambda x2: row_copy(ends, far, e_send_row, e_recv, x2, me).wait_send())
+
+    def relayed(zr):
+        for dx in range(1, cols):
+            relay_copy(vals, v_rel, v_recv, zr, dx).wait_send()
+            relay_copy(far, e_rel, e_recv, zr, dx).wait_send()
+    loop(0, z, relayed)
+
+    def handed(zr):
+        to_next(passed.at[zr], far, e_send, e_recv, zr).wait_send()
+        to_next(v_ref, vals, v_send, v_recv, zr).wait_send()
+
+    @pl.when(more)
+    def _():
+        loop(0, z + 1, handed)
     for dh in range(1, peers):
         for c in range(chunks):
             part_copy(dh, c).wait_send()
@@ -263,34 +357,39 @@
     chunks = 2
     many = per_group * tok
     vmem = pl.BlockSpec(memory_space=pltpu.VMEM)
+    hbm = pl.BlockSpec(memory_space=pltpu.HBM)
     dma = pltpu.SemaphoreType.DMA
     body = functools.partial(kernel, n, cols, peers, groups, per_group, chunks)
+    inputs = (queries, keys, values, house, beta, out_weight)
     return pl.pallas_call(
         body,
         out_shape=jax.ShapeDtypeStruct((tok, width), bf16),
-        in_specs=[vmem] * 5 + [pl.BlockSpec(memory_space=pl.ANY)],
+        in_specs=[hbm] * len(inputs),
         out_specs=vmem,
-        scratch_shapes=[
-            pltpu.VMEM(out_weight.shape, bf16),
-            pltpu.VMEM((groups * HD, HD + tok), bf16),
-            pltpu.VMEM((n, groups * HD, HD + tok), bf16),
+        scratch_shapes=[pltpu.VMEM(one.shape, one.dtype) for one in inputs] + [
+            pltpu.VMEM((groups * HD, tok), bf16),
+            pltpu.VMEM((cols, groups * HD, HD), bf16),
+            pltpu.VMEM((n, groups * HD, tok), bf16),
+            pltpu.VMEM((rows, groups * HD, tok), bf16),
             pltpu.VMEM((n,) + values.shape, bf16),
             pltpu.VMEM((groups, many, HD), bf16),
+            pltpu.VMEM((groups, HD, HD), f32),
             pltpu.VMEM((groups, HD, HD), f32),
             pltpu.VMEM((groups, many, tok), f32),
             pltpu.VMEM((groups, many, tok), f32),
             pltpu.VMEM((groups, many, HD), f32),
             pltpu.VMEM((peers - 1, tok, width), bf16),
             pltpu.VMEM((peers - 1, tok, width), bf16),
-            dma((peers,)),
+            dma((len(inputs) - 1,)), dma((peers,)),
             dma((rows,)), dma((cols,)), dma((rows, cols)), dma((n,)),
+            dma((cols,)), dma((cols,)),
             dma((rows,)), dma((cols,)), dma((rows, cols)), dma((n,)),
             dma((peers - 1, chunks)), dma((peers - 1, chunks)),
         ],
         compiler_params=pltpu.CompilerParams(
-            collective_id=0, has_side_effects=True, vmem_limit_bytes=48 * 2**20
+            collective_id=0, has_side_effects=True, vmem_limit_bytes=63 * 2**20
         ),
-    )(queries, keys, values, house, beta, out_weight)
+    )(*inputs)
 
 
 def solution(mesh):

time: 41.7 us -> 36.1 us (0.87)
  the two profiles are of different devices: /device:TPU:25 before, /device:TPU:27 now
where the time goes in v2:
time: 36.1 us; the launch traced here: 35.9 us
  Pallas kernels  34.3 us (95%)
  local copies, waits for them, and re-layouts  1.67 us (5%)
    pallas_call x1, Pallas kernels, per_device(): pl.pallas_call(body, out_shape=jax.ShapeDtypeStruct((tok, width), bf16),...  34.3 us
    unnamed x1, local copies, waits for them, and re-layouts  1.67 us

profile of v2, /device:TPU:27, one launch (start us, length us, event | category | flops | bytes accessed | tf_op | source)
XLA Modules:
  0.0 35.9 jit_solution(11694786865772218513)
XLA Ops:
  0.0 34.3 %shard_map.64 = bf16[128,1024]{1,0:T(8,128)(2,1)} custom-call(bf16[128,1024]{1,0:T(8,128)(2,1)} %refs_0_.1, bf16[128,256]{1,0:T(8,128)(2,1)} %refs_1_.1, bf16[128,256]{1,0:T(8,128)(2,1)} %refs_2_.1, bf16[128,256]{1,0:T(8,128)(2,1)} %refs_3_.1, f32[2,128]{1,0:T(2,128)} %refs_4_.1, bf16[1024,2048]{1,0:T(8,128)(2,1)} %refs_5_.1), custom_call_target="tpu_custom_call" | custom-call | tf_op jit(solution)/shard_map/pallas_call | solution.py:364
  34.3 1.7 %copy.8 = bf16[128,1024]{1,0:T(8,128)(2,1)} copy(bf16[128,1024]{1,0:T(8,128)(2,1)} %shard_map.64) | data formatting | bytes 524288

commit v3 on v2

--- a/solution.py
+++ b/solution.py
@@ -255,21 +255,7 @@
                 passed[zr, under(g), :] = moved.astype(bf16)
             to_next(passed.at[zr], far, e_send, e_recv, zr).start()
 
-    def absorb(i):
-        block = me - 1 - i
-        zr = lax.div(block, cols)
-        xr = lax.rem(block, cols)
-        earlier = zr < z
-
-        @pl.when(earlier & (xr == cols - 1))
-        def _():
-            relay_keys(zr)
-
-        @pl.when(jnp.logical_not(earlier & (xr == x)))
-        def _():
-            wait_block(vals, v_recv, block)
-            wait_block(far, e_recv, block)
-
+    def absorb(block):
         for g in span:
             moved = dot_two(*split(prod_ref[g]), far[block, under(g), :])
             score = dot(turned_ref[g], moved.astype(bf16)) * scale
@@ -281,12 +267,38 @@
             sum_ref[g] = sum_ref[g] * shrink + expo
             acc_ref[g] = acc_ref[g] * shrink + dot(expo.astype(bf16), vals[block, :, lanes(g)])
 
-        @pl.when(jnp.logical_not(earlier))
-        def _():
-            for g in span:
-                prod_ref[g] = dot_two(*split(prod_ref[g]), maps[xr, under(g), :])
-
-    loop(0, me, absorb)
+    def same_row(i):
+        xr = x - 1 - i
+        wait_block(vals, v_recv, z * cols + xr)
+        wait_block(far, e_recv, z * cols + xr)
+        absorb(z * cols + xr)
+        for g in span:
+            prod_ref[g] = dot_two(*split(prod_ref[g]), maps[xr, under(g), :])
+
+    def earlier_row(i):
+        zr = z - 1 - i
+
+        def one(j):
+            block = zr * cols + lax.rem(x + j, cols)
+
+            @pl.when(j == min(1, cols - 1))
+            def _():
+                @pl.when(zr > 0)
+                def _():
+                    relay_keys(zr - 1)
+
+            @pl.when(j > 0)
+            def _():
+                wait_block(vals, v_recv, block)
+                wait_block(far, e_recv, block)
+            absorb(block)
+        loop(0, cols, one)
+
+    @pl.when(z > 0)
+    def _():
+        relay_keys(z - 1)
+    loop(0, x, same_row)
+    loop(0, z, earlier_row)
 
     pieces = []
     for g in span:
@@ -363,7 +375,7 @@
     inputs = (queries, keys, values, house, beta, out_weight)
     return pl.pallas_call(
         body,
-        out_shape=jax.ShapeDtypeStruct((tok, width), bf16),
+        out_shape=jax.ShapeDtypeStruct((tok, width), f32),
         in_specs=[hbm] * len(inputs),
         out_specs=vmem,
         scratch_shapes=[pltpu.VMEM(one.shape, one.dtype) for one in inputs] + [
@@ -389,7 +401,7 @@
         compiler_params=pltpu.CompilerParams(
             collective_id=0, has_side_effects=True, vmem_limit_bytes=63 * 2**20
         ),
-    )(*inputs)
+    )(*inputs).astype(bf16)
 
 
 def solution(mesh):

time: 36.1 us -> 33.4 us (0.925)
  the two profiles are of different devices: /device:TPU:27 before, /device:TPU:25 now
where the time goes in v3:
time: 33.4 us; the launch traced here: 33.2 us
  Pallas kernels  31.4 us (94%)
  other arithmetic  1.78 us (5%)
    pallas_call x1, Pallas kernels, per_device(): pl.pallas_call(body, out_shape=jax.ShapeDtypeStruct((tok, width), f32), i...  31.4 us
    convert_element_type x1, other arithmetic, per_device(): return pl.pallas_call(body, out_shape=jax.ShapeDtypeStruct((tok, width),...  1.78 us

profile of v3, /device:TPU:25, one launch (start us, length us, event | category | flops | bytes accessed | tf_op | source)
XLA Modules:
  0.0 33.2 jit_solution(5819937455565921895)
XLA Ops:
  0.0 31.4 %shard_map.64 = f32[128,1024]{1,0:T(8,128)} custom-call(bf16[128,1024]{1,0:T(8,128)(2,1)} %refs_0_.1, bf16[128,256]{1,0:T(8,128)(2,1)} %refs_1_.1, bf16[128,256]{1,0:T(8,128)(2,1)} %refs_2_.1, bf16[128,256]{1,0:T(8,128)(2,1)} %refs_3_.1, f32[2,128]{1,0:T(2,128)} %refs_4_.1, bf16[1024,2048]{1,0:T(8,128)(2,1)} %refs_5_.1), custom_call_target="tpu_custom_call" | custom-call | tf_op jit(solution)/shard_map/pallas_call | solution.py:376
  31.4 1.8 %convert_element_type.3 = bf16[128,1024]{1,0:T(8,128)(2,1)} convert(f32[128,1024]{1,0:T(8,128)} %shard_map.64) | non-fusion elementwise | flops 131072 | bytes 786432 | tf_op jit(solution)/shard_map/convert_element_type | solution.py:404

commit v4 on v3

--- a/solution.py
+++ b/solution.py
@@ -255,10 +255,9 @@
                 passed[zr, under(g), :] = moved.astype(bf16)
             to_next(passed.at[zr], far, e_send, e_recv, zr).start()
 
-    def absorb(block):
+    def absorb(block, keys_of):
         for g in span:
-            moved = dot_two(*split(prod_ref[g]), far[block, under(g), :])
-            score = dot(turned_ref[g], moved.astype(bf16)) * scale
+            score = dot(turned_ref[g], keys_of(g)) * scale
             old = max_ref[g]
             top = jnp.maximum(old, jnp.max(score, 1, keepdims=True))
             shrink = jnp.exp2(old - top)
@@ -271,7 +270,11 @@
         xr = x - 1 - i
         wait_block(vals, v_recv, z * cols + xr)
         wait_block(far, e_recv, z * cols + xr)
-        absorb(z * cols + xr)
+
+        def carried(g):
+            moved = dot_two(*split(prod_ref[g]), far[z * cols + xr, under(g), :])
+            return moved.astype(bf16)
+        absorb(z * cols + xr, carried)
         for g in span:
             prod_ref[g] = dot_two(*split(prod_ref[g]), maps[xr, under(g), :])
 
@@ -291,13 +294,18 @@
             def _():
                 wait_block(vals, v_recv, block)
                 wait_block(far, e_recv, block)
-            absorb(block)
+            absorb(block, lambda g: far[block, under(g), :])
         loop(0, cols, one)
 
     @pl.when(z > 0)
     def _():
         relay_keys(z - 1)
     loop(0, x, same_row)
+
+    @pl.when((z > 0) & (x > 0))
+    def _():
+        for g in span:
+            turned_ref[g] = map_times(turned_ref[g], prod_ref[g]).astype(bf16)
     loop(0, z, earlier_row)
 
     pieces = []
@@ -375,7 +383,7 @@
     inputs = (queries, keys, values, house, beta, out_weight)
     return pl.pallas_call(
         body,
-        out_shape=jax.ShapeDtypeStruct((tok, width), f32),
+        out_shape=jax.ShapeDtypeStruct((tok, width), bf16),
         in_specs=[hbm] * len(inputs),
         out_specs=vmem,
         scratch_shapes=[pltpu.VMEM(one.shape, one.dtype) for one in inputs] + [
@@ -401,7 +409,7 @@
         compiler_params=pltpu.CompilerParams(
             collective_id=0, has_side_effects=True, vmem_limit_bytes=63 * 2**20
         ),
-    )(*inputs).astype(bf16)
+    )(*inputs)
 
 
 def solution(mesh):

time: 33.4 us -> 32.1 us (0.961)
  other arithmetic: 1.78 us -> 0 us
  local copies, waits for them, and re-layouts: 0 us -> 1.67 us
  Pallas kernels: 31.4 us -> 30.3 us
    convert_element_type x1 -> x0, other arithmetic: 1.78 us -> none  [per_device(): return pl.pallas_call(body, out_shape=jax.ShapeDtypeStruct((tok, width),...]
    unnamed x0 -> x1, local copies, waits for them, and re-layouts: none -> 1.67 us
    pallas_call x1, Pallas kernels: 31.4 us -> 30.3 us  [per_device(): pl.pallas_call(body, out_shape=jax.ShapeDtypeStruct((tok, width), bf16),...]
where the time goes in v4:
time: 32.1 us; the launch traced here: 32 us
  Pallas kernels  30.3 us (94%)
  local copies, waits for them, and re-layouts  1.67 us (5%)
    pallas_call x1, Pallas kernels, per_device(): pl.pallas_call(body, out_shape=jax.ShapeDtypeStruct((tok, width), bf16),...  30.3 us
    unnamed x1, local copies, waits for them, and re-layouts  1.67 us

profile of v4, /device:TPU:25, one launch (start us, length us, event | category | flops | bytes accessed | tf_op | source)
XLA Modules:
  0.0 32.0 jit_solution(7410952710048475875)
XLA Ops:
  0.0 30.3 %shard_map.64 = bf16[128,1024]{1,0:T(8,128)(2,1)} custom-call(bf16[128,1024]{1,0:T(8,128)(2,1)} %refs_0_.1, bf16[128,256]{1,0:T(8,128)(2,1)} %refs_1_.1, bf16[128,256]{1,0:T(8,128)(2,1)} %refs_2_.1, bf16[128,256]{1,0:T(8,128)(2,1)} %refs_3_.1, f32[2,128]{1,0:T(2,128)} %refs_4_.1, bf16[1024,2048]{1,0:T(8,128)(2,1)} %refs_5_.1), custom_call_target="tpu_custom_call" | custom-call | tf_op jit(solution)/shard_map/pallas_call | solution.py:384
  30.3 1.7 %copy.8 = bf16[128,1024]{1,0:T(8,128)(2,1)} copy(bf16[128,1024]{1,0:T(8,128)(2,1)} %shard_map.64) | data formatting | bytes 524288
